TPU v7x, 32 devices: a whole 2x2x4 slice. The times are simulated.
32 devices in a mesh: seq: 8 (over y, x, core), dp: 4 (over z).
Axes of the slice: x: 2, y: 2, z: 4, core: 2. Of those that a mesh axis runs over, the one named last changes fastest.
Arguments:
- queries: bfloat16 [4, 4096, 1024], P('dp', 'seq'), may hold values from -6 to 6
- key_rows: bfloat16 [4, 4096, 1024], P('dp', 'seq'), may hold values from -6 to 6
- value_rows: bfloat16 [4, 4096, 1024], P('dp', 'seq'), may hold values from -6 to 6
- gate_rows: bfloat16 [4, 4096, 1024], P('dp', 'seq'), may hold values from -6 to 6
- cotangent: bfloat16 [4, 4096, 1024], P('dp', 'seq'), may hold values from -6 to 6
- far_blocks: int32 [4, 32, 4], P('dp'), may hold values from 0 to 31, as said below
- treated: int32 [4, 32], P('dp'), may hold values 0 or 1
- norm_gain: float32 [1024], replicated, may hold values from 0.1 to 1.9
- out_weight: bfloat16 [1024, 1024], replicated, may hold values from -0.1875 to 0.1875
Outputs:
- output: bfloat16 [4, 4096, 1024], P('dp', 'seq')
- grad_queries: bfloat16 [4, 4096, 1024], P('dp', 'seq')
- grad_keys: bfloat16 [4, 4096, 1024], P('dp', 'seq')
- grad_values: bfloat16 [4, 4096, 1024], P('dp', 'seq')
- grad_gate: bfloat16 [4, 4096, 1024], P('dp', 'seq')
- grad_weight: float32 [1024, 1024], P(('seq', 'dp'))
- grad_gain: float32 [1024], replicated
Inputs may be any that keep to these rules, and one draw needn't show every extreme that they name: `far_blocks`: every entry names a block of the same history that is held by another index of seq than its query block. Of the 16 entries of the query blocks held by index s of seq, 3 name blocks of index (s + o) mod 8 for o = 1 and o = 2, and 2 for each other o from 3 to 7; which entries these are, and which block of that index, are drawn.
All inputs are finite; a program needn't handle non-finite values. No bound on the sum of `treated` on one device may be relied on, other than what follows from the above.
Results may differ from a plain program's by a relative error of at most 0.0065.
Values may be sent and summed in bfloat16 or wider, within the bound.
A program may use at most 192 MiB of HBM per device.

v0:
```python
import jax
import jax.numpy as jnp
from jax import lax
from jax.sharding import PartitionSpec as P

HEADS = 8
HEAD_DIM = 128
BLK = 128
FAR = 4
epsilon = 1e-05


def from_behind(value, axis, by):
    peers = lax.axis_size(axis)
    pairs = [(i, i + by) for i in range(peers) if 0 <= i + by < peers]
    return lax.ppermute(value, axis, pairs)


def to_heads(rows):
    return rows.reshape(rows.shape[:-1] + (HEADS, rows.shape[-1] // HEADS))


def as_bf16(values):
    return values.astype(jnp.bfloat16)


def pair_scores(query_part, key_part):
    scores = jnp.einsum(
        "pqhd,pkhd->phqk",
        to_heads(query_part),
        to_heads(key_part),
        preferred_element_type=jnp.float32,
    )
    return scores * HEAD_DIM ** (-0.5)


def pair_forward(query_part, key_part, value_part, pair_mask):
    weights = as_bf16(jax.nn.silu(pair_scores(query_part, key_part)) * pair_mask[:, None])
    result = jnp.einsum(
        "phqk,pkhd->pqhd", weights, to_heads(value_part), preferred_element_type=jnp.float32
    )
    return result.reshape(query_part.shape)


def pair_backward(query_part, key_part, value_part, grad_part, pair_mask):
    scores = pair_scores(query_part, key_part)
    logistic = jax.nn.sigmoid(scores)
    weights = as_bf16(jax.nn.silu(scores) * pair_mask[:, None])
    grad_heads = to_heads(grad_part)
    grad_weights = jnp.einsum(
        "pqhd,pkhd->phqk", grad_heads, to_heads(value_part), preferred_element_type=jnp.float32
    )
    grad_value = jnp.einsum(
        "phqk,pqhd->pkhd", weights, grad_heads, preferred_element_type=jnp.float32
    )
    grad_scores = as_bf16(
        grad_weights
        * logistic
        * (1.0 + scores * (1.0 - logistic))
        * pair_mask[:, None]
        * HEAD_DIM ** (-0.5)
    )
    grad_query = jnp.einsum(
        "phqk,pkhd->pqhd", grad_scores, to_heads(key_part), preferred_element_type=jnp.float32
    )
    grad_key = jnp.einsum(
        "phqk,pqhd->pkhd", grad_scores, to_heads(query_part), preferred_element_type=jnp.float32
    )
    row_shape = query_part.shape
    return (
        grad_query.reshape(row_shape),
        grad_key.reshape(row_shape),
        grad_value.reshape(row_shape),
    )


def far_plan(far_all, my_index, seq_count, blocks, capacity):
    block_ids = far_all.reshape(seq_count, blocks * FAR)
    owners = block_ids // blocks
    local_ids = block_ids % blocks
    positions = jnp.arange(blocks * FAR)
    same_owner = owners[:, :, None] == owners[:, None, :]
    before = positions[None, :] < positions[:, None]
    slot_rank = jnp.sum(same_owner & before[None], axis=2)
    slot_ids = jnp.arange(capacity)
    send_hit = (owners[:, None, :] == my_index) & (slot_rank[:, None, :] == slot_ids[None, :, None])
    all_local = jnp.sum(jnp.where(send_hit, local_ids[:, None, :], 0), axis=2).reshape(-1)
    all_ok = jnp.any(send_hit, axis=2).reshape(-1)
    my_owners = lax.dynamic_index_in_dim(owners, my_index, 0, keepdims=False)
    my_ranks = lax.dynamic_index_in_dim(slot_rank, my_index, 0, keepdims=False)
    slot_count = seq_count * capacity
    read_at = my_owners * capacity + my_ranks
    back_hit = read_at[None, :] == jnp.arange(slot_count)[:, None]
    return (all_local, all_ok, read_at, back_hit)


def body(
    queries, key_rows, value_rows, gate_rows, cotangent, far_blocks, treated, norm_gain, out_weight
):
    width = queries.shape[2]
    blocks = queries.shape[1] // BLK
    seq_count = lax.axis_size("seq")
    my_index = lax.axis_index("seq")
    requests = blocks * FAR
    capacity = (requests + seq_count - 2) // (seq_count - 1)
    slot_count = seq_count * capacity
    query_blocks = queries[0].reshape(blocks, BLK, width)
    key_blocks = key_rows[0].reshape(blocks, BLK, width)
    value_blocks = value_rows[0].reshape(blocks, BLK, width)
    both_blocks = jnp.concatenate([key_blocks, value_blocks], axis=2)
    from_prev = from_behind(both_blocks[blocks - 1], "seq", 1)
    prev_both = jnp.concatenate([from_prev[None], both_blocks[:-1]], axis=0)
    prev_keys = prev_both[:, :, :width]
    prev_values = prev_both[:, :, width:]
    causal = jnp.tril(jnp.ones((BLK, BLK), jnp.float32))[None]
    all_ones = jnp.ones((1, BLK, BLK), jnp.float32)
    all_local, all_ok, read_at, back_hit = far_plan(
        far_blocks[0], my_index, seq_count, blocks, capacity
    )
    block_ids = lax.dynamic_slice_in_dim(far_blocks[0], my_index * blocks, blocks, 0).reshape(
        requests
    )
    far_mask = treated[0][block_ids].astype(jnp.float32)[:, None, None]
    far_queries = jnp.repeat(query_blocks, FAR, axis=0)
    back_matrix = back_hit.astype(jnp.bfloat16)
    local_onehot = ((all_local[None, :] == jnp.arange(blocks)[:, None]) & all_ok[None, :]).astype(
        jnp.bfloat16
    )
    diag_out = pair_forward(query_blocks, key_blocks, value_blocks, causal)
    prev_out = pair_forward(query_blocks, prev_keys, prev_values, all_ones)
    send_both = jnp.where(
        all_ok[:, None, None], both_blocks[all_local], jnp.zeros((), jnp.bfloat16)
    )
    got_both = lax.all_to_all(
        send_both.reshape(seq_count, capacity, BLK, 2 * width),
        "seq",
        split_axis=0,
        concat_axis=0,
        tiled=True,
    )
    received = got_both.reshape(slot_count, BLK, 2 * width)
    far_both = received[read_at]
    far_keys = far_both[:, :, :width]
    far_values = far_both[:, :, width:]
    far_terms = as_bf16(pair_forward(far_queries, far_keys, far_values, far_mask))
    far_sum = (
        lax.optimization_barrier(far_terms)
        .astype(jnp.float32)
        .reshape(blocks, FAR, BLK, width)
        .sum(axis=1)
    )
    attention = (diag_out + prev_out + far_sum).reshape(blocks * BLK, width)
    centered = attention - jnp.mean(attention, axis=1, keepdims=True)
    inv_std = lax.rsqrt(jnp.mean(centered * centered, axis=1, keepdims=True) + epsilon)
    normed = centered * inv_std
    gate_vals = gate_rows[0].astype(jnp.float32)
    mixed = as_bf16(normed * norm_gain * gate_vals)
    output = jnp.dot(mixed, out_weight, preferred_element_type=jnp.float32).astype(jnp.bfloat16)
    grad_in = cotangent[0]
    grad_mixed = lax.dot_general(
        grad_in, out_weight, (((1,), (1,)), ((), ())), preferred_element_type=jnp.float32
    )
    grad_weight = lax.psum_scatter(
        lax.dot_general(
            mixed, grad_in, (((0,), (0,)), ((), ())), preferred_element_type=jnp.float32
        ),
        ("seq", "dp"),
        scatter_dimension=0,
        tiled=True,
    )
    grad_gate = as_bf16(grad_mixed * normed * norm_gain)
    scaled = grad_mixed * gate_vals
    grad_gain = lax.psum(jnp.sum(scaled * normed, axis=0), ("seq", "dp"))
    grad_hat = scaled * norm_gain
    grad_attn = inv_std * (
        grad_hat
        - jnp.mean(grad_hat, axis=1, keepdims=True)
        - normed * jnp.mean(grad_hat * normed, axis=1, keepdims=True)
    )
    grad_blocks = as_bf16(grad_attn).reshape(blocks, BLK, width)
    dq_diag, dk_diag, dv_diag = pair_backward(
        query_blocks, key_blocks, value_blocks, grad_blocks, causal
    )
    dq_prev, dk_prev, dv_prev = pair_backward(
        query_blocks, prev_keys, prev_values, grad_blocks, all_ones
    )
    prev_terms = lax.optimization_barrier(as_bf16(jnp.concatenate([dk_prev, dv_prev], axis=2)))
    from_next = from_behind(prev_terms[0], "seq", -1)
    next_terms = jnp.concatenate([prev_terms[1:], from_next[None]], axis=0).astype(jnp.float32)
    far_grads = jnp.repeat(grad_blocks, FAR, axis=0)
    dq_far, dk_far, dv_far = pair_backward(far_queries, far_keys, far_values, far_grads, far_mask)
    query_terms = as_bf16(dq_far)
    back_terms = as_bf16(jnp.concatenate([dk_far, dv_far], axis=2))
    send_back = jnp.dot(
        back_matrix, back_terms.reshape(requests, -1), preferred_element_type=jnp.float32
    )
    send_back = as_bf16(send_back).reshape(slot_count, BLK, 2 * width)
    got_back = lax.all_to_all(
        send_back.reshape(seq_count, capacity, BLK, 2 * width),
        "seq",
        split_axis=0,
        concat_axis=0,
        tiled=True,
    )
    owned_terms = got_back.reshape(slot_count, BLK * 2 * width)
    far_query = (
        lax.optimization_barrier(query_terms)
        .astype(jnp.float32)
        .reshape(blocks, FAR, BLK, width)
        .sum(axis=1)
    )
    owned_sum = jnp.dot(
        local_onehot, lax.optimization_barrier(owned_terms), preferred_element_type=jnp.float32
    )
    owned_sum = owned_sum.reshape(blocks, BLK, 2 * width)
    rows = blocks * BLK
    grad_queries = as_bf16(dq_diag + dq_prev + far_query).reshape(1, rows, width)
    key_total = jnp.concatenate([dk_diag, dv_diag], axis=2) + next_terms + owned_sum
    grad_keys = as_bf16(key_total[:, :, :width]).reshape(1, rows, width)
    grad_values = as_bf16(key_total[:, :, width:]).reshape(1, rows, width)
    return (
        output[None],
        grad_queries,
        grad_keys,
        grad_values,
        grad_gate[None],
        grad_weight,
        grad_gain,
    )


def solution(mesh):
    in_specs = (
        P("dp", "seq", None),
        P("dp", "seq", None),
        P("dp", "seq", None),
        P("dp", "seq", None),
        P("dp", "seq", None),
        P("dp", None, None),
        P("dp", None),
        P(),
        P(),
    )
    out_specs = (
        P("dp", "seq", None),
        P("dp", "seq", None),
        P("dp", "seq", None),
        P("dp", "seq", None),
        P("dp", "seq", None),
        P(("seq", "dp"), None),
        P(),
    )
    return jax.shard_map(body, mesh=mesh, in_specs=in_specs, out_specs=out_specs, check_vma=False)
```

profile of v0, /device:TPU:0, one launch (start us, length us, event | category | flops | bytes accessed | tf_op | source)
XLA Modules:
  0.0 594.2 jit_solution(34854243904092478)
XLA Ops:
  9.1 3.1 pad_maximum_fusion.1
  12.2 7.5 %gather_fusion = bf16[24,128,2048]{2,1,0:T(8,128)(2,1)} fusion(bf16[4,128,2048]{2,1,0:T(8,128)(2,1)} %pad_maximum_fusion.1, s32[1024]{0:T(1024)S(1)} %pad_clamp_fusion.2), kind=kCustom, calls=%fused_computation | custom fusion | bytes 25165920 | tf_op jit(solution)/shard_map/gather | solution.py:132
  19.7 10.6 %broadcast_select_fusion = bf16[8,3,128,2048]{3,2,1,0:T(8,128)(2,1)} fusion(bf16[8,3,128,2048]{3,2,1,0:T(8,128)(2,1)} %bitcast.251, pred[8,3]{1,0:T(8,128)(4,1)S(1)} %copy.282), kind=kLoop, calls=%fused_computation.4 | loop fusion | flops 6291456 | bytes 25165848 | tf_op jit(solution)/shard_map/jit(_where)/select_n | solution.py:131
  30.3 5.5 all-to-all-start
  35.8 1.8 fusion.48
  37.6 3.2 collective-permute-start
  45.4 2.8 fusion.29
  48.2 2.2 fusion.45
  50.4 2.6 fusion.36
  53.7 2.5 copy.336
  56.2 2.3 copy.286
  58.4 4.4 fusion.40
  62.8 2.5 pad_maximum_fusion.3
  65.3 2.3 copy.275
  67.6 2.3 copy.274
  69.8 3.1 fusion.75
  73.0 102.6 %all-to-all-done = bf16[8,3,128,2048]{3,2,1,0:T(8,128)(2,1)} async-done(((bf16[8,3,128,2048]{3,2,1,0:T(8,128)(2,1)}), bf16[8,3,128,2048]{3,2,1,0:T(8,128)(2,1)}, u32[]{:S(2)}, u32[]{:S(2)}) %all-to-all-start) | async-done | bytes 12582944 | tf_op jit(solution)/shard_map/all_to_all | solution.py:134
  175.6 9.5 %gather_fusion.1 = bf16[16,128,2048]{2,1,0:T(8,128)(2,1)} fusion(bf16[24,128,2048]{2,1,0:T(8,128)(2,1)} %bitcast.11, s32[1024]{0:T(1024)S(1)} %pad_clamp_fusion.1), kind=kCustom, calls=%fused_computation.1 | custom fusion | bytes 16777280 | tf_op jit(solution)/shard_map/gather | solution.py:142
  185.1 6.1 %fusion.73 = (bf16[16,128,1024]{2,1,0:T(8,128)(2,1)}, bf16[16,128,1024]{2,1,0:T(8,128)(2,1)}) fusion(bf16[16,128,2048]{2,1,0:T(8,128)(2,1)} %gather_fusion.1), kind=kLoop, calls=%fused_computation.143 | loop fusion | bytes 16777216 | tf_op jit(solution)/shard_map/slice | solution.py:143
  191.1 6.4 %copy.285 = bf16[16,128,1024]{1,2,0:T(8,128)(2,1)} copy(bf16[16,128,1024]{2,1,0:T(8,128)(2,1)} %get-tuple-element.18) | data formatting | bytes 8388608 | tf_op jit(solution)/shard_map/slice | solution.py:143
  197.6 6.3 %copy.284 = bf16[16,128,1024]{1,2,0:T(8,128)(2,1)} copy(bf16[16,128,1024]{2,1,0:T(8,128)(2,1)} %get-tuple-element.19) | data formatting | bytes 8388608 | tf_op jit(solution)/shard_map/slice | solution.py:144
  203.8 2.2 broadcast_in_dim.78
  206.3 5.6 fusion.4
  213.9 2.0 convert_reduce_fusion.1
  215.9 3.1 copy.292
  219.0 5.4 fusion.71
  224.6 2.9 copy.280
  227.5 4.6 fusion.31
  235.0 2.3 copy.300
  237.3 2.2 broadcast_in_dim.80
  239.8 5.0 convolution_convert_fusion.1
  244.8 12.7 %fusion.9 = bf16[16,8,128,128]{2,3,1,0:T(8,128)(2,1)} fusion(f32[16,8,128,128]{3,2,1,0:T(8,128)} %get-tuple-element.29, f32[16]{0:T(128)S(1)} %convert_element_type.121, bf16[16,128,8,128]{1,3,2,0:T(8,128)(2,1)} %bitcast.258, bf16[16,128,8,128]{1,3,2,0:T(8,128)(2,1)} %bitcast.261), kind=kOutput, calls=%fused_computation.20 | convolution fusion | flops 562036736 | bytes 20971584 | tf_op jit(solution)/shard_map/pqhd,pkhd->phqk/dot_general | solution.py:50
  257.4 6.7 %copy.315 = bf16[16,128,1024]{2,1,0:T(8,128)(2,1)} copy(bf16[16,128,1024]{1,2,0:T(8,128)(2,1)} %bitcast.263) | data formatting | bytes 8388608 | tf_op jit(solution)/shard_map/reshape | solution.py:73
  264.1 8.4 %convolution_convert_fusion.2 = bf16[16,8,128,128]{2,3,1,0:T(8,128)(2,1)} fusion(bf16[16,8,128,128]{2,3,1,0:T(8,128)(2,1)} %fusion.9, bf16[16,128,8,128]{1,3,2,0:T(8,128)(2,1)} %bitcast.256), kind=kOutput, calls=%fused_computation.26 | convolution fusion | flops 538968064 | bytes 12582912 | tf_op jit(solution)/shard_map/phqk,pqhd->pkhd/dot_general | solution.py:66
  272.5 6.4 %copy.314 = bf16[16,128,1024]{2,1,0:T(8,128)(2,1)} copy(bf16[16,128,1024]{1,2,0:T(8,128)(2,1)} %bitcast.265) | data formatting | bytes 8388608 | tf_op jit(solution)/shard_map/reshape | solution.py:72
  279.0 8.3 %pad_maximum_fusion = bf16[16,128,2048]{2,1,0:T(8,128)(2,1)} fusion(bf16[16,128,1024]{2,1,0:T(8,128)(2,1)} %copy.315, bf16[16,128,1024]{2,1,0:T(8,128)(2,1)} %copy.314), kind=kLoop, calls=%fused_computation.5 | loop fusion | flops 16777216 | bytes 16777216 | tf_op jit(solution)/shard_map/concatenate | solution.py:193
  287.3 11.3 %copy.339 = bf16[2,8,128,2048]{3,1,2,0:T(8,128)(2,1)} copy(bf16[2,8,128,2048]{3,2,1,0:T(8,128)(2,1)} %bitcast.252) | data formatting | bytes 16777216
  298.6 11.4 %convolution_convert_fusion = bf16[24,262144]{1,0:T(8,128)(2,1)} fusion(bf16[16,262144]{1,0:T(8,128)(2,1)} %bitcast.249, s32[16]{0:T(128)S(1)} %bitcast.300), kind=kOutput, calls=%fused_computation.3 | convolution fusion | flops 207618432 | bytes 20971584 | tf_op jit(solution)/shard_map/dot_general | solution.py:194
  309.9 14.7 %copy.340 = bf16[3,8,128,2048]{3,2,1,0:T(8,128)(2,1)} copy(bf16[3,8,128,2048]{3,1,2,0:T(8,128)(2,1)} %bitcast.247) | data formatting | bytes 25165824
  324.6 17.8 %all-to-all-start.1 = ((bf16[8,3,128,2048]{3,2,1,0:T(8,128)(2,1)}), bf16[8,3,128,2048]{3,2,1,0:T(8,128)(2,1)}, u32[]{:S(2)}, u32[]{:S(2)}) async-start(bf16[8,3,128,2048]{3,2,1,0:T(8,128)(2,1)} %bitcast.250), calls=%async_computation.1 | async-start | bytes 25165824 | tf_op jit(solution)/shard_map/all_to_all | solution.py:198
  342.4 2.6 copy.319
  345.0 4.3 fusion.18
  349.3 2.3 copy.320
  351.6 4.9 fusion.34
  357.2 2.5 copy.338
  359.7 2.4 copy.307
  362.1 3.4 fusion.28
  374.8 2.5 copy.299
  377.3 2.7 add.206
  380.1 2.7 slice.56
  382.7 1.9 slice_bitcast_fusion
  386.1 4.7 convolution_convert_fusion.3
  390.8 2.0 convert_reduce_fusion
  392.8 2.9 copy.305
  395.8 147.2 %psum.7 = f32[1024]{0:T(1024)} all-reduce(f32[1024]{0:T(1024)S(1)} %get-tuple-element.7), channel_id=1, replica_groups=mesh['seq'=8,'dp'=4] {'seq','dp'}, use_global_device_ids=true, to_apply=%region_11.12 | all-reduce | flops 1024 | bytes 8192 | tf_op jit(solution)/shard_map/psum | solution.py:173
  543.0 3.1 fusion.76
  548.4 2.2 fusion.30
  550.6 2.2 fusion.69
  552.9 11.7 %copy.341 = bf16[3,8,128,2048]{3,1,2,0:T(8,128)(2,1)S(1)} copy(bf16[3,8,128,2048]{3,2,1,0:T(8,128)(2,1)} %bitcast.95) | data formatting | bytes 25165824
  564.6 3.3 fusion.56
  567.8 4.5 copy.354
  572.3 5.4 copy.316
  577.7 4.6 fusion.11
  583.4 2.3 copy.318
  (117 shorter events, 29.0 us)
Async XLA Ops:
  7.2 43.2 %copy-start = (bf16[1024,1024]{1,0:T(8,128)(2,1)S(1)}, bf16[1024,1024]{1,0:T(8,128)(2,1)}, u32[]{:S(2)}) copy-start(bf16[1024,1024]{1,0:T(8,128)(2,1)} %param.17) | copy-start | bytes 6291460
  9.0 3.2 copy-start.30
  30.3 5.5 copy-start.11
  30.3 145.3 %all-to-all-start = ((bf16[8,3,128,2048]{3,2,1,0:T(8,128)(2,1)}), bf16[8,3,128,2048]{3,2,1,0:T(8,128)(2,1)}, u32[]{:S(2)}, u32[]{:S(2)}) async-start(bf16[8,3,128,2048]{3,2,1,0:T(8,128)(2,1)} %broadcast_select_fusion), calls=%async_computation | async-start | bytes 25165824 | tf_op jit(solution)/shard_map/all_to_all | solution.py:134
  35.8 5.0 copy-start.32
  37.6 25.2 %collective-permute-start = (bf16[128,2048]{1,0:T(8,128)(2,1)}, bf16[128,2048]{1,0:T(8,128)(2,1)}, u32[]{:S(2)}, u32[]{:S(2)}) collective-permute-start(bf16[128,2048]{1,0:T(8,128)(2,1)} %fusion.48), channel_id=1, source_target_pairs={{0,4},{4,8},{8,12},{12,16},{16,20},{20,24},{24,28},{1,5},{5,9},{9,... | collective-permute-start | bytes 1572872 | tf_op jit(solution)/shard_map/ppermute | solution.py:16
  41.0 1.3 copy-start.20
  45.3 2.8 copy-start.14
  48.2 2.2 copy-start.28
  50.4 2.6 copy-start.1
  58.4 4.4 copy-start.19
  203.8 2.5 copy-start.9
  206.0 5.9 copy-start.7
  206.3 5.6 copy-start.10
  212.0 2.0 copy-start.5
  224.6 2.9 copy-start.29
  227.5 4.6 copy-start.4
  227.5 4.6 copy-start.12
  232.1 1.3 copy-start.2
  237.3 2.5 copy-start.6
  239.4 5.3 copy-start.8
  324.6 228.2 %all-to-all-start.1 = ((bf16[8,3,128,2048]{3,2,1,0:T(8,128)(2,1)}), bf16[8,3,128,2048]{3,2,1,0:T(8,128)(2,1)}, u32[]{:S(2)}, u32[]{:S(2)}) async-start(bf16[8,3,128,2048]{3,2,1,0:T(8,128)(2,1)} %bitcast.250), calls=%async_computation.1 | async-start | bytes 25165824 | tf_op jit(solution)/shard_map/all_to_all | solution.py:198
  342.4 244.6 %reduce-scatter.2.cloned.1.call-start = ((), (), s32[]{:S(2)}) async-start(), calls=%async_computation.3 | async-start | bytes 4325376 | tf_op jit(solution)/shard_map/reduce_scatter | solution.py:163
  356.4 0.7 copy-start.31
  365.5 1.6 copy-start.24
  365.5 1.9 copy-start.26
  368.3 2.3 copy-start.22
  368.3 2.6 copy-start.25
  370.9 1.4 copy-start.15
  372.3 1.0 copy-start.21
  372.3 1.6 copy-start.16
  384.6 193.1 %collective-permute-start.1 = (bf16[128,2048]{0,1:T(8,128)(2,1)}, bf16[128,2048]{0,1:T(8,128)(2,1)}, u32[]{:S(2)}, u32[]{:S(2)}) collective-permute-start(bf16[128,2048]{0,1:T(8,128)(2,1)} %slice_bitcast_fusion), channel_id=1, source_target_pairs={{4,0},{8,4},{12,8},{16,12},{20,16},{24,20},{28,24},{5,1},{9,5},{13... | collective-permute-start | bytes 1572872 | tf_op jit(solution)/shard_map/ppermute | solution.py:16
  543.0 3.1 copy-start.17
  543.0 3.1 copy-start.18
  546.1 2.0 copy-start.3
  546.1 2.2 copy-start.13
  548.4 2.3 copy-start.23
  548.4 2.3 copy-start.27
Sparse Core Ops, SparseCore 0:
  356.6 152.8 reduce-scatter.1
where the time goes:
time: 606 us; the launch traced here: 594 us
  local copies, waits for them, and re-layouts  159 us (26%)
  blocking collectives  147 us (24%)
  waiting for transfers between devices  103 us (17%)
  matrix products  89.9 us (15%)
  other arithmetic  52.6 us (9%)
  starting transfers between devices  27.9 us (5%)
  between operations  14.8 us (2%)
    psum x1, blocking collectives, body(): grad_gain = lax.psum(jnp.sum(scaled * normed, axis=0), ('seq', 'dp'))  147 us
    all_to_all x1, waiting for transfers between devices, body(): lax.all_to_all(send_both.reshape(seq_count, capacity, BLK, 2 * width), 's...  103 us
    unnamed x75, local copies, waits for them, and re-layouts  57.6 us
    all_to_all x1, starting transfers between devices, body(): lax.all_to_all(send_back.reshape(seq_count, capacity, BLK, 2 * width), 's...  17.8 us
    dot_general x3, matrix products, pair_backward(): jnp.einsum('pqhd,pkhd->phqk', grad_heads, to_heads(value_part), preferred...  17.5 us
    slice x2, local copies, waits for them, and re-layouts, body(): far_keys = far_both[:, :, :width]  12.5 us
  transfers between devices with their start and end apart: 5, of which 1 were waited for; matrix products, arithmetic and copies ran while one was open for 21% of the time, Pallas kernels for 0%

commit v1 on v0

--- a/solution.py
+++ b/solution.py
@@ -8,6 +8,28 @@
 BLK = 128
 FAR = 4
 epsilon = 1e-05
+
+
+def split_up(value, dim, size):
+    before, after = (value.shape[:dim], value.shape[dim + 1 :])
+    return jnp.moveaxis(value.reshape(*before, size, -1, *after), dim, 0)
+
+
+def laid_out(blocks, dim):
+    blocks = jnp.moveaxis(blocks, 0, dim)
+    shape = blocks.shape
+    return blocks.reshape(*shape[:dim], shape[dim] * shape[dim + 1], *shape[dim + 2 :])
+
+
+def exchange_directly(x, axis, split_dim, concat_dim):
+    peers, place = (lax.axis_size(axis), lax.axis_index(axis))
+    blocks = split_up(x, split_dim, peers)
+    finished = [blocks[place]]
+    for lap in range(1, peers):
+        sent = blocks[(place + lap) % peers]
+        finished.append(lax.ppermute(sent, axis, [(i, (i + lap) % peers) for i in range(peers)]))
+    blocks = jnp.stack(finished)[(place - jnp.arange(peers)) % peers]
+    return laid_out(blocks, concat_dim)
 
 
 def from_behind(value, axis, by):
@@ -195,12 +217,8 @@
         back_matrix, back_terms.reshape(requests, -1), preferred_element_type=jnp.float32
     )
     send_back = as_bf16(send_back).reshape(slot_count, BLK, 2 * width)
-    got_back = lax.all_to_all(
-        send_back.reshape(seq_count, capacity, BLK, 2 * width),
-        "seq",
-        split_axis=0,
-        concat_axis=0,
-        tiled=True,
+    got_back = exchange_directly(
+        send_back.reshape(seq_count, capacity, BLK, 2 * width), "seq", 0, 0
     )
     owned_terms = got_back.reshape(slot_count, BLK * 2 * width)
     far_query = (

time: 606 us -> 706 us (1.17)
  the two profiles are of different devices: /device:TPU:0 before, /device:TPU:3 now
where the time goes in v1:
time: 706 us; the launch traced here: 695 us
  waiting for transfers between devices  199 us (28%)
  local copies, waits for them, and re-layouts  184 us (26%)
  blocking collectives  132 us (19%)
  matrix products  92.1 us (13%)
  other arithmetic  51.7 us (7%)
  starting transfers between devices  21.7 us (3%)
  between operations  14.7 us (2%)
    psum x1, blocking collectives, body(): grad_gain = lax.psum(jnp.sum(scaled * normed, axis=0), ('seq', 'dp'))  132 us
    ppermute x2, waiting for transfers between devices, from_behind(): return lax.ppermute(value, axis, pairs)  110 us
    ppermute x7, waiting for transfers between devices, exchange_directly(): lax.ppermute(sent, axis, [(i, (i + lap) % peers) for i in range(peers)])  89 us
    unnamed x103, local copies, waits for them, and re-layouts  63.5 us
    dot_general x3, matrix products, pair_backward(): jnp.einsum('pqhd,pkhd->phqk', grad_heads, to_heads(value_part), preferred...  19.5 us
  transfers between devices with their start and end apart: 11, of which 3 were waited for; matrix products, arithmetic and copies ran while one was open for 20% of the time, Pallas kernels for 0%

profile of v1, /device:TPU:3, one launch (start us, length us, event | category | flops | bytes accessed | tf_op | source)
XLA Modules:
  0.0 694.7 jit_solution(7742643810599705089)
XLA Ops:
  10.0 3.1 pad_maximum_fusion.1
  13.1 7.5 %gather_fusion = bf16[24,128,2048]{2,1,0:T(8,128)(2,1)} fusion(bf16[4,128,2048]{2,1,0:T(8,128)(2,1)} %pad_maximum_fusion.1, s32[1024]{0:T(1024)S(1)} %get-tuple-element.40), kind=kCustom, calls=%fused_computation | custom fusion | bytes 25165920 | tf_op jit(solution)/shard_map/gather | solution.py:154
  20.6 10.7 %broadcast_select_fusion = bf16[8,3,128,2048]{3,2,1,0:T(8,128)(2,1)} fusion(bf16[8,3,128,2048]{3,2,1,0:T(8,128)(2,1)} %bitcast.283, pred[8,3]{1,0:T(8,128)(4,1)S(1)} %copy.282), kind=kLoop, calls=%fused_computation.5 | loop fusion | flops 6291456 | bytes 25165848 | tf_op jit(solution)/shard_map/jit(_where)/select_n | solution.py:153
  31.3 5.5 all-to-all-start
  38.6 3.6 collective-permute-start
  47.1 2.7 fusion.29
  52.0 2.7 fusion.36
  56.5 2.5 copy.336
  59.0 2.3 copy.286
  61.3 2.5 copy.319
  63.8 4.4 fusion.40
  68.2 109.8 %collective-permute-done = bf16[128,2048]{1,0:T(8,128)(2,1)} collective-permute-done((bf16[128,2048]{1,0:T(8,128)(2,1)}, bf16[128,2048]{1,0:T(8,128)(2,1)}, u32[]{:S(2)}, u32[]{:S(2)}) %collective-permute-start) | collective-permute-done | bytes 524320 | tf_op jit(solution)/shard_map/ppermute | solution.py:38
  178.0 2.5 pad_maximum_fusion.3
  180.6 2.3 copy.275
  182.8 2.3 copy.274
  185.1 3.1 fusion.77
  188.2 9.3 %gather_fusion.1 = bf16[16,128,2048]{2,1,0:T(8,128)(2,1)} fusion(bf16[24,128,2048]{2,1,0:T(8,128)(2,1)} %bitcast.11, s32[1024]{0:T(1024)S(1)} %pad_clamp_fusion.2), kind=kCustom, calls=%fused_computation.1 | custom fusion | bytes 16777280 | tf_op jit(solution)/shard_map/gather | solution.py:164
  197.5 6.1 fusion.75
  203.7 6.4 copy.285
  210.0 6.4 copy.284
  218.9 5.5 fusion.4
  228.5 3.3 copy.292
  231.9 5.4 fusion.73
  237.5 2.9 copy.280
  240.4 4.6 fusion.31
  249.2 2.4 copy.307
  251.6 4.5 fusion.28
  258.0 2.3 multiply_convert_fusion.1
  260.4 2.4 copy.300
  265.3 5.0 convolution_convert_fusion.1
  270.3 12.7 %fusion.9 = bf16[16,8,128,128]{2,3,1,0:T(8,128)(2,1)} fusion(f32[16,8,128,128]{3,2,1,0:T(8,128)} %get-tuple-element.37, f32[16]{0:T(128)S(1)} %convert_element_type.121, bf16[16,128,8,128]{1,3,2,0:T(8,128)(2,1)} %bitcast.291, bf16[16,128,8,128]{1,3,2,0:T(8,128)(2,1)} %bitcast.294), kind=kOutput, calls=%fused_computation.21 | convolution fusion | flops 562036736 | bytes 20971584 | tf_op jit(solution)/shard_map/pqhd,pkhd->phqk/dot_general | solution.py:72
  283.0 8.6 %convolution_convert_fusion.2 = bf16[16,8,128,128]{2,3,1,0:T(8,128)(2,1)} fusion(bf16[16,8,128,128]{2,3,1,0:T(8,128)(2,1)} %fusion.9, bf16[16,128,8,128]{1,3,2,0:T(8,128)(2,1)} %bitcast.289), kind=kOutput, calls=%fused_computation.27 | convolution fusion | flops 538968064 | bytes 12582912 | tf_op jit(solution)/shard_map/phqk,pqhd->pkhd/dot_general | solution.py:88
  291.6 3.4 convolution_convert_fusion.3
  297.4 2.3 copy.320
  305.6 2.6 copy.299
  308.2 2.7 add.294
  310.9 6.4 copy.315
  317.2 4.5 convert_reduce_fusion
  321.7 2.9 copy.305
  324.7 6.8 copy.314
  331.4 8.2 %pad_maximum_fusion = bf16[16,128,2048]{2,1,0:T(8,128)(2,1)} fusion(bf16[16,128,1024]{2,1,0:T(8,128)(2,1)} %copy.315, bf16[16,128,1024]{2,1,0:T(8,128)(2,1)} %copy.314), kind=kLoop, calls=%fused_computation.6 | loop fusion | flops 16777216 | bytes 16777216 | tf_op jit(solution)/shard_map/concatenate | solution.py:215
  339.7 11.4 %copy.339 = bf16[2,8,128,2048]{3,1,2,0:T(8,128)(2,1)} copy(bf16[2,8,128,2048]{3,2,1,0:T(8,128)(2,1)} %bitcast.285) | data formatting | bytes 16777216
  351.0 3.3 fusion.34
  354.4 11.3 %convolution_convert_fusion = bf16[24,262144]{1,0:T(8,128)(2,1)} fusion(bf16[16,262144]{1,0:T(8,128)(2,1)} %bitcast.281, s32[16]{0:T(128)S(1)} %bitcast.334), kind=kOutput, calls=%fused_computation.4 | convolution fusion | flops 207618432 | bytes 20971584 | tf_op jit(solution)/shard_map/dot_general | solution.py:216
  365.6 11.7 %copy.340 = bf16[3,8,128,2048]{3,2,1,0:T(8,128)(2,1)S(1)} copy(bf16[3,8,128,2048]{3,1,2,0:T(8,128)(2,1)} %bitcast.279) | data formatting | bytes 25165824
  377.3 5.6 dynamic-slice_bitcast_fusion
  383.0 2.7 collective-permute-start.4
  388.0 2.3 fusion.30
  397.9 131.7 %psum.7 = f32[1024]{0:T(1024)} all-reduce(f32[1024]{0:T(1024)S(1)} %get-tuple-element.7), channel_id=1, replica_groups=mesh['seq'=8,'dp'=4] {'seq','dp'}, use_global_device_ids=true, to_apply=%region_11.12 | all-reduce | flops 1024 | bytes 8192 | tf_op jit(solution)/shard_map/psum | solution.py:195
  529.7 3.9 fusion.71
  534.9 2.7 bitcast_dynamic-update-slice_fusion.6
  537.6 2.9 collective-permute-start.6
  540.5 2.7 bitcast_dynamic-update-slice_fusion.5
  544.2 2.8 bitcast_dynamic-update-slice_fusion.4
  546.9 71.0 %collective-permute-done.5 = bf16[1,3,128,2048]{3,2,1,0:T(8,128)(2,1)S(1)} collective-permute-done((bf16[1,3,128,2048]{3,2,1,0:T(8,128)(2,1)S(1)}, bf16[1,3,128,2048]{3,2,1,0:T(8,128)(2,1)S(1)}, u32[]{:S(2)}, u32[]{:S(2)}) %collective-permute-start.5) | collective-permute-done | bytes 1572896 | tf_op jit(solution)/shard_map/ppermute | solution.py:30
  619.2 18.0 %collective-permute-done.6 = bf16[1,3,128,2048]{3,2,1,0:T(8,128)(2,1)S(1)} collective-permute-done((bf16[1,3,128,2048]{3,2,1,0:T(8,128)(2,1)S(1)}, bf16[1,3,128,2048]{3,2,1,0:T(8,128)(2,1)S(1)}, u32[]{:S(2)}, u32[]{:S(2)}) %collective-permute-start.6) | collective-permute-done | bytes 1572896 | tf_op jit(solution)/shard_map/ppermute | solution.py:30
  639.8 2.8 bitcast_dynamic-update-slice_fusion
  642.6 11.1 %gather_fusion.3 = bf16[8,3,128,2048]{3,2,1,0:T(8,128)(2,1)} fusion(bf16[8,3,128,2048]{3,2,1,0:T(8,128)(2,1)} %bitcast.309, s32[1024]{0:T(1024)} %pad_clamp_fusion), kind=kCustom, calls=%fused_computation.3 | custom fusion | bytes 25165856 | tf_op jit(solution)/shard_map/gather | solution.py:31
  653.7 11.7 %copy.341 = bf16[3,8,128,2048]{3,1,2,0:T(8,128)(2,1)S(1)} copy(bf16[3,8,128,2048]{3,2,1,0:T(8,128)(2,1)} %bitcast.284) | data formatting | bytes 25165824
  665.4 3.3 fusion.56
  668.6 4.4 copy.354
  673.1 5.4 copy.316
  678.5 4.6 fusion.11
  684.1 2.3 copy.318
  (162 shorter events, 55.7 us)
Async XLA Ops:
  7.2 44.8 %copy-start = (bf16[1024,1024]{1,0:T(8,128)(2,1)S(1)}, bf16[1024,1024]{1,0:T(8,128)(2,1)}, u32[]{:S(2)}) copy-start(bf16[1024,1024]{1,0:T(8,128)(2,1)} %param.17) | copy-start | bytes 6291460
  31.3 5.5 copy-start.14
  31.3 156.9 %all-to-all-start = ((bf16[8,3,128,2048]{3,2,1,0:T(8,128)(2,1)}), bf16[8,3,128,2048]{3,2,1,0:T(8,128)(2,1)}, u32[]{:S(2)}, u32[]{:S(2)}) async-start(bf16[8,3,128,2048]{3,2,1,0:T(8,128)(2,1)} %broadcast_select_fusion), calls=%async_computation | async-start | bytes 25165824 | tf_op jit(solution)/shard_map/all_to_all | solution.py:156
  36.8 650.9 %reduce-scatter.2.cloned.1.call-start = ((), (), s32[]{:S(2)}) async-start(), calls=%async_computation.2 | async-start | bytes 4325376 | tf_op jit(solution)/shard_map/reduce_scatter | solution.py:185
  38.6 139.4 %collective-permute-start = (bf16[128,2048]{1,0:T(8,128)(2,1)}, bf16[128,2048]{1,0:T(8,128)(2,1)}, u32[]{:S(2)}, u32[]{:S(2)}) collective-permute-start(bf16[128,2048]{1,0:T(8,128)(2,1)} %fusion.48), channel_id=1, source_target_pairs={{0,4},{4,8},{8,12},{12,16},{16,20},{20,24},{24,28},{1,5},{5,9},{9,... | collective-permute-start | bytes 1572872 | tf_op jit(solution)/shard_map/ppermute | solution.py:38
  42.2 1.3 copy-start.27
  46.5 3.4 copy-start.18
  49.8 2.2 copy-start.39
  52.0 3.9 copy-start.1
  63.8 114.2 %copy-start.25 = (bf16[3,128,2048]{2,1,0:T(8,128)(2,1)S(1)}, bf16[3,128,2048]{2,1,0:T(8,128)(2,1)}, u32[]{:S(2)}) copy-start(bf16[3,128,2048]{2,1,0:T(8,128)(2,1)} %fusion.29) | copy-start | bytes 4718596
  216.4 2.5 copy-start.11
  218.6 5.9 copy-start.9
  218.9 5.6 copy-start.13
  224.5 2.0 copy-start.6
  237.5 2.9 copy-start.41
  240.4 4.6 copy-start.2
  240.4 4.6 copy-start.15
  245.0 1.3 copy-start.3
  246.9 1.0 copy-start.17
  251.6 4.5 copy-start.31
  251.6 4.5 copy-start.35
  256.1 1.9 copy-start.30
  256.1 1.9 copy-start.37
  262.8 2.5 copy-start.7
  265.0 5.4 copy-start.10
  283.0 8.6 %copy-start.8 = (bf16[16,8,128,128]{2,3,1,0:T(8,128)(2,1)S(1)}, bf16[16,8,128,128]{2,3,1,0:T(8,128)(2,1)}, u32[]{:S(2)}) copy-start(bf16[16,8,128,128]{2,3,1,0:T(8,128)(2,1)} %fusion.9) | copy-start | bytes 12582916
  283.0 8.6 %copy-start.12 = (bf16[16,128,1024]{1,2,0:T(8,128)(2,1)S(1)}, bf16[16,128,1024]{1,2,0:T(8,128)(2,1)}, u32[]{:S(2)}) copy-start(bf16[16,128,1024]{1,2,0:T(8,128)(2,1)} %copy.285) | copy-start | bytes 12582916
  291.6 3.4 copy-start.5
  291.6 3.4 copy-start.23
  291.6 4.3 copy-start.24
  299.6 2.1 copy-start.28
  301.7 1.2 copy-start.19
  302.9 1.2 copy-start.38
  339.6 11.4 %copy-start.26 = (bf16[4,128,1024]{2,1,0:T(8,128)(2,1)S(1)}, bf16[4,128,1024]{2,1,0:T(8,128)(2,1)}, u32[]{:S(2)}) copy-start(bf16[4,128,1024]{2,1,0:T(8,128)(2,1)} %copy.320) | copy-start | bytes 3145732
  339.6 11.4 %copy-start.40 = (bf16[1,512,1024]{2,1,0:T(8,128)(2,1)S(1)}, bf16[1,512,1024]{2,1,0:T(8,128)(2,1)}, u32[]{:S(2)}) copy-start(bf16[1,512,1024]{2,1,0:T(8,128)(2,1)} %param.13) | copy-start | bytes 3145732
  377.3 9.9 %copy-start.20 = (bf16[4,128,2048]{1,2,0:T(8,128)(2,1)S(1)}, bf16[4,128,2048]{1,2,0:T(8,128)(2,1)}, u32[]{:S(2)}) copy-start(bf16[4,128,2048]{1,2,0:T(8,128)(2,1)} %pad_maximum_fusion.2) | copy-start | bytes 6291460
  377.3 10.7 %copy-start.4 = (f32[512,1024]{1,0:T(8,128)S(1)}, f32[512,1024]{1,0:T(8,128)}, u32[]{:S(2)}) copy-start(f32[512,1024]{1,0:T(8,128)} %copy-done.3) | copy-start | bytes 6291460
  377.3 10.7 %copy-start.16 = (bf16[1,512,1024]{2,1,0:T(8,128)(2,1)S(1)}, bf16[1,512,1024]{2,1,0:T(8,128)(2,1)}, u32[]{:S(2)}) copy-start(bf16[1,512,1024]{2,1,0:T(8,128)(2,1)} %param.12) | copy-start | bytes 3145732
  383.0 160.3 %collective-permute-start.4 = (bf16[1,3,128,2048]{3,2,1,0:T(8,128)(2,1)}, bf16[1,3,128,2048]{3,2,1,0:T(8,128)(2,1)}, u32[]{:S(2)}, u32[]{:S(2)}) collective-permute-start(bf16[1,3,128,2048]{3,2,1,0:T(8,128)(2,1)} %get-tuple-element.22), channel_id=1, source_target_pairs={{0,12},{4,16},{8,20},{12,24},{16,28},{20,0},{24,4},{28,8},{1,13},{... | collective-permute-start | bytes 4718600 | tf_op jit(solution)/shard_map/ppermute | solution.py:30
  385.7 152.0 %collective-permute-start.3 = (bf16[1,3,128,2048]{3,2,1,0:T(8,128)(2,1)}, bf16[1,3,128,2048]{3,2,1,0:T(8,128)(2,1)}, u32[]{:S(2)}, u32[]{:S(2)}) collective-permute-start(bf16[1,3,128,2048]{3,2,1,0:T(8,128)(2,1)} %get-tuple-element.23), channel_id=1, source_target_pairs={{0,8},{4,12},{8,16},{12,20},{16,24},{20,28},{24,0},{28,4},{1,9},{5... | collective-permute-start | bytes 4718600 | tf_op jit(solution)/shard_map/ppermute | solution.py:30
  385.7 147.9 %collective-permute-start.2 = (bf16[1,3,128,2048]{3,2,1,0:T(8,128)(2,1)}, bf16[1,3,128,2048]{3,2,1,0:T(8,128)(2,1)}, u32[]{:S(2)}, u32[]{:S(2)}) collective-permute-start(bf16[1,3,128,2048]{3,2,1,0:T(8,128)(2,1)} %get-tuple-element.24), channel_id=1, source_target_pairs={{0,4},{4,8},{8,12},{12,16},{16,20},{20,24},{24,28},{28,0},{1,5},{5... | collective-permute-start | bytes 4718600 | tf_op jit(solution)/shard_map/ppermute | solution.py:30
  388.0 2.3 copy-start.21
  388.0 2.3 copy-start.22
  390.3 1.3 copy-start.29
  393.3 136.3 %copy-start.36 = (bf16[4,128,8,128]{1,3,2,0:T(8,128)(2,1)S(1)}, bf16[4,128,8,128]{1,3,2,0:T(8,128)(2,1)}, u32[]{:S(2)}) copy-start(bf16[4,128,8,128]{1,3,2,0:T(8,128)(2,1)} %copy.307) | copy-start | bytes 3145732
  394.6 283.9 %collective-permute-start.1 = (bf16[128,2048]{0,1:T(8,128)(2,1)}, bf16[128,2048]{0,1:T(8,128)(2,1)}, u32[]{:S(2)}, u32[]{:S(2)}) collective-permute-start(bf16[128,2048]{0,1:T(8,128)(2,1)} %slice_bitcast_fusion), channel_id=1, source_target_pairs={{4,0},{8,4},{12,8},{16,12},{20,16},{24,20},{28,24},{5,1},{9,5},{13... | collective-permute-start | bytes 1572872 | tf_op jit(solution)/shard_map/ppermute | solution.py:38
  396.5 243.3 %collective-permute-start.8 = (bf16[1,3,128,2048]{3,2,1,0:T(8,128)(2,1)}, bf16[1,3,128,2048]{3,2,1,0:T(8,128)(2,1)}, u32[]{:S(2)}, u32[]{:S(2)}) collective-permute-start(bf16[1,3,128,2048]{3,2,1,0:T(8,128)(2,1)} %get-tuple-element.18), channel_id=1, source_target_pairs={{0,28},{4,0},{8,4},{12,8},{16,12},{20,16},{24,20},{28,24},{1,29},{... | collective-permute-start | bytes 4718600 | tf_op jit(solution)/shard_map/ppermute | solution.py:30
  529.7 3.9 copy-start.34
  533.6 4.0 copy-start.33
  533.6 84.4 %collective-permute-start.5 = (bf16[1,3,128,2048]{3,2,1,0:T(8,128)(2,1)S(1)}, bf16[1,3,128,2048]{3,2,1,0:T(8,128)(2,1)S(1)}, u32[]{:S(2)}, u32[]{:S(2)}) collective-permute-start(bf16[1,3,128,2048]{3,2,1,0:T(8,128)(2,1)S(1)} %copy-done.34), channel_id=1, source_target_pairs={{0,16},{4,20},{8,24},{12,28},{16,0},{20,4},{24,8},{28,12},{1,17},{... | collective-permute-start | bytes 4718600 | tf_op jit(solution)/shard_map/ppermute | solution.py:30
  537.6 5.6 copy-start.32
  537.6 99.6 %collective-permute-start.6 = (bf16[1,3,128,2048]{3,2,1,0:T(8,128)(2,1)S(1)}, bf16[1,3,128,2048]{3,2,1,0:T(8,128)(2,1)S(1)}, u32[]{:S(2)}, u32[]{:S(2)}) collective-permute-start(bf16[1,3,128,2048]{3,2,1,0:T(8,128)(2,1)S(1)} %copy-done.33), channel_id=1, source_target_pairs={{0,20},{4,24},{8,28},{12,0},{16,4},{20,8},{24,12},{28,16},{1,21},{... | collective-permute-start | bytes 4718600 | tf_op jit(solution)/shard_map/ppermute | solution.py:30
  543.2 95.3 %collective-permute-start.7 = (bf16[1,3,128,2048]{3,2,1,0:T(8,128)(2,1)S(1)}, bf16[1,3,128,2048]{3,2,1,0:T(8,128)(2,1)S(1)}, u32[]{:S(2)}, u32[]{:S(2)}) collective-permute-start(bf16[1,3,128,2048]{3,2,1,0:T(8,128)(2,1)S(1)} %copy-done.32), channel_id=1, source_target_pairs={{0,24},{4,28},{8,0},{12,4},{16,8},{20,12},{24,16},{28,20},{1,25},{... | collective-permute-start | bytes 4718600 | tf_op jit(solution)/shard_map/ppermute | solution.py:30
  653.7 11.7 %copy-start.42 = (s32[24]{0:T(128)S(1)}, s32[24]{0:T(128)}, u32[]{:S(2)}) copy-start(s32[24]{0:T(128)} %eq.87) | copy-start | bytes 292
  653.7 11.7 %copy-start.43 = (pred[24]{0:T(512)(128)(4,1)S(1)}, pred[24]{0:T(512)(128)(4,1)}, u32[]{:S(2)}) copy-start(pred[24]{0:T(512)(128)(4,1)} %and.119) | copy-start | bytes 76
Sparse Core Ops, SparseCore 0:
  354.5 145.7 reduce-scatter.1
